TPU v7x, 32 devices: a whole 2x2x4 slice. The times are simulated.
32 devices in a mesh: tensor: 8 (over z, y), context: 4 (over x, core).
Axes of the slice: x: 2, y: 2, z: 4, core: 2. Of those that a mesh axis runs over, the one named last changes fastest.
Arguments:
- tokens: bfloat16 [1536, 8192], P('context'), may hold values from -48 to 48
- w_query: bfloat16 [8192, 1024], P(None, 'tensor'), may hold values from -0.0625 to 0.0625
- w_key: bfloat16 [8192, 1024], P(None, 'tensor'), may hold values from -0.0625 to 0.0625
- w_value: bfloat16 [8192, 1024], P(None, 'tensor'), may hold values from -0.0625 to 0.0625
- mix_gate: bfloat16 [8, 16], replicated, may hold values from -2 to 2
- mix_up: bfloat16 [8, 16], replicated, may hold values from -2 to 2
- mix_down: bfloat16 [16, 8], replicated, may hold values from -1.5 to 1.5
- block_ids: int32 [16], P('context'), may hold values from 0 to 7, as said below
Outputs:
- attended: bfloat16 [1536, 1024], P('context', 'tensor')
Inputs may be any that keep to these rules, and one draw needn't show every extreme that they name: `block_ids`: device c of the context axis holds entries 4c to 4c+3: (a, 7 - a) for the first sequence and (b, 7 - b) for the second; over all devices each sequence's block numbers appear once each.
All inputs are finite; a program needn't handle non-finite values.
Results may differ from a plain program's by a relative error of at most 0.012.
The roundings to bfloat16 on the way count: a program that leaves them out, or rounds other values in their place, can miss the bound.
Values may be sent and summed in bfloat16 or wider, within the bound.
A program may use at most 64 MiB of HBM per device.

v0:
```python
import jax
import jax.numpy as jnp
from jax import lax
from jax.sharding import PartitionSpec as P

HEAD_DIM = 128
BLK = 96


def mix_exchanged(gathered, mix_gate, mix_up, mix_down):
    gate_part = jnp.einsum("hnc,hf->ncf", gathered, mix_gate, preferred_element_type=jnp.float32)
    up_part = jnp.einsum("hnc,hf->ncf", gathered, mix_up, preferred_element_type=jnp.float32)
    hidden = (jax.nn.silu(gate_part) * up_part).astype(jnp.bfloat16)
    mixing = jnp.einsum("ncf,fh->hnc", hidden, mix_down, preferred_element_type=jnp.float32)
    return (gathered.astype(jnp.float32) + mixing).astype(jnp.bfloat16)


def shards(tokens, w_query, w_key, w_value, mix_gate, mix_up, mix_down, block_ids):
    query_rows = jnp.dot(tokens, w_query, preferred_element_type=jnp.float32).astype(jnp.bfloat16)
    key_rows = jnp.dot(tokens, w_key, preferred_element_type=jnp.float32).astype(jnp.bfloat16)
    value_rows = jnp.dot(tokens, w_value, preferred_element_type=jnp.float32).astype(jnp.bfloat16)
    local_count = tokens.shape[0]
    local_offsets = jnp.arange(local_count, dtype=jnp.int32)
    query_pos = (
        jnp.repeat(block_ids, BLK, total_repeat_length=local_count) * BLK + local_offsets % BLK
    )
    query_seq = local_offsets // BLK % 4 // 2
    block_all = lax.all_gather(block_ids, "context", axis=0, tiled=True)
    mixed_here = mix_exchanged(
        lax.all_to_all(value_rows[None], "tensor", split_axis=1, concat_axis=0, tiled=True),
        mix_gate,
        mix_up,
        mix_down,
    )
    mixed_rows = lax.all_to_all(mixed_here, "tensor", split_axis=0, concat_axis=1, tiled=True)[0]
    scale = HEAD_DIM ** (-0.5)
    running_max = jnp.full((local_count,), -1e30, jnp.float32)
    running_total = jnp.zeros((local_count,), jnp.float32)
    running_sum = jnp.zeros((local_count, query_rows.shape[1]), jnp.float32)
    key_piece = lax.all_gather(key_rows, "context", axis=0, tiled=True)
    value_piece = lax.all_gather(mixed_rows, "context", axis=0, tiled=True)
    count = key_piece.shape[0]
    offsets = jnp.arange(count, dtype=jnp.int32)
    key_pos = jnp.repeat(block_all, BLK, total_repeat_length=count) * BLK + offsets % BLK
    key_seq = offsets // BLK % 4 // 2
    allowed = (query_seq[:, None] == key_seq[None, :]) & (key_pos[None, :] <= query_pos[:, None])
    scores = (
        lax.dot_general(
            query_rows, key_piece, (((1,), (1,)), ((), ())), preferred_element_type=jnp.float32
        )
        * scale
    )
    scores = jnp.where(allowed, scores, -1e30)
    new_max = jnp.maximum(running_max, jnp.max(scores, axis=1))
    correction = jnp.exp(running_max - new_max)
    weights = jnp.where(allowed, jnp.exp(scores - new_max[:, None]), 0.0)
    new_total = running_total * correction + jnp.sum(weights, axis=1)
    new_sum = running_sum * correction[:, None] + jnp.dot(
        weights.astype(jnp.bfloat16), value_piece, preferred_element_type=jnp.float32
    )
    return (new_sum / new_total[:, None]).astype(jnp.bfloat16)


def solution(mesh):
    in_specs = (
        P("context", None),
        P(None, "tensor"),
        P(None, "tensor"),
        P(None, "tensor"),
        P(),
        P(),
        P(),
        P("context"),
    )
    out_specs = P("context", "tensor")
    return jax.shard_map(shards, mesh=mesh, in_specs=in_specs, out_specs=out_specs, check_vma=False)
```

profile of v0, /device:TPU:1, one launch (start us, length us, event | category | flops | bytes accessed | tf_op | source)
XLA Modules:
  0.0 80.6 jit_solution(8789265267908995261)
XLA Ops:
  0.0 5.4 %fusion.13 = bf16[1,384,128]{2,1,0:T(8,128)(2,1)S(1)} fusion(bf16[384,8192]{1,0:T(8,128)(2,1)} %param.12, bf16[8192,128]{1,0:T(8,128)(2,1)} %param.15), kind=kOutput, calls=%fused_computation.17 | convolution fusion | flops 805355520 | bytes 8486912 | tf_op jit(solution)/shard_map/dot_general | solution.py:21
  5.4 0.2 copy.28
  5.5 0.5 broadcast.456
  6.1 1.2 %reduce.4 = bf16[384,128]{1,0:T(8,128)(2,1)S(1)} reduce(bf16[384,1,128]{2,1,0:T(2,128)(2,1)S(1)} %bitcast.53, bf16[]{:T(256)} %broadcast.456), dimensions={1}, to_apply=%bitcast.52.reduce_sub_computation | reduce | bytes 196610
  7.3 0.7 reshape.320
  7.9 6.4 %all-to-all-start = ((bf16[8,2,3072]{2,1,0:T(2,128)(2,1)}), bf16[8,2,3072]{2,1,0:T(2,128)(2,1)S(1)}, u32[]{:S(2)}, u32[]{:S(2)}) async-start(bf16[8,2,3072]{2,1,0:T(2,128)(2,1)} %reshape.320), calls=%async_computation | async-start | bytes 196608 | tf_op jit(solution)/shard_map/all_to_all | solution.py:30
  14.4 0.7 fusion.59
  15.0 0.7 dynamic-slice.12
  16.4 0.2 dynamic-update-slice.6
  16.6 4.8 %all-reduce = s32[16]{0:T(128)S(1)} all-reduce(s32[16]{0:T(128)S(1)} %dynamic-update-slice.6), channel_id=1, replica_groups=mesh['tensor'=8,'context'=4] {'context'}, use_global_device_ids=true, to_apply=%add | all-reduce | flops 16 | bytes 128
  21.4 0.7 fusion.60
  22.4 5.2 %convolution_convert_fusion.1 = bf16[384,128]{1,0:T(8,128)(2,1)S(1)} fusion(bf16[384,8192]{1,0:T(8,128)(2,1)} %param.12, bf16[8192,128]{1,0:T(8,128)(2,1)} %param.14), kind=kOutput, calls=%fused_computation.15 | convolution fusion | flops 805355520 | bytes 8486912 | tf_op jit(solution)/shard_map/dot_general | solution.py:20
  27.6 7.1 %all_gather.10 = bf16[1536,128]{1,0:T(8,128)(2,1)S(1)} all-gather(bf16[384,128]{1,0:T(8,128)(2,1)S(1)} %convolution_convert_fusion.1), channel_id=1, replica_groups=mesh['tensor'=8,'context'=4] {'context'}, dimensions={0}, use_global_device_ids=true | all-gather | bytes 491520 | tf_op jit(solution)/shard_map/all_gather | solution.py:40
  34.7 2.5 %add_select_fusion.3 = (s32[384]{0:T(512)S(1)}, s32[384]{0:T(512)S(1)}) fusion(pred[384]{0:T(512)(128)(4,1)S(1)} %copy-done.18, pred[384]{0:T(512)(128)(4,1)S(1)} %copy-done.19, pred[384]{0:T(512)(128)(4,1)S(1)} %copy-done.20, s32[]{:T(128)} %bitcast.20, s32[]{:T(128)} %bitcast.19, s32[]{:T(128)} %bitcast.18, s32[]{:T(128)} %bitcast.17), kind=kLoop, calls=%fused_computation.60 | loop fusion | flops 16512 | bytes 4240 | tf_op jit(solution)/shard_map/jit(floor_divide)/jit(_where)/select_n | solution.py:27
  37.4 10.1 %fusion.38 = s32[1536]{0:T(1024)S(1)} fusion(pred[1536]{0:T(1024)(128)(4,1)S(1)} %copy-done.3, pred[1536]{0:T(1024)(128)(4,1)S(1)} %copy-done.4, pred[1536]{0:T(1024)(128)(4,1)S(1)} %copy-done.5, pred[1536]{0:T(1024)(128)(4,1)S(1)} %copy-done.6, pred[1536]{0:T(1024)(128)(4,1)S(1)} %copy-done.7, pred[1536]{0:T(1024)(128)(4,1)S(1)} %copy-done.8, ...), kind=kLoop, calls=%fused_computation.48 | loop fusion | flops 35328 | bytes 29248 | tf_op jit(solution)/shard_map/add | solution.py:44
  47.5 6.9 %fusion.61 = (f32[384]{0:T(512)S(1)}, f32[384,1536]{1,0:T(8,128)}) fusion(bf16[1536,128]{1,0:T(8,128)(2,1)S(1)} %all_gather.10, bf16[384,8192]{1,0:T(8,128)(2,1)} %param.12, bf16[8192,128]{1,0:T(8,128)(2,1)S(1)} %copy-done, s32[384]{0:T(512)S(1)} %get-tuple-element.54, s32[1536]{0:T(1024)S(1)} %fusion.38, s32[1536]{0:T(1024)S(1)} %add_select_fusion, ...), kind=kOutput, calls=%fused_computation.87 | convolution fusion | flops 959889024 | bytes 11158016 | tf_op jit(solution)/shard_map/dot_general | solution.py:48
  54.4 2.5 %fusion.1 = f32[384]{0:T(512)S(1)} fusion(f32[384,1536]{1,0:T(8,128)} %get-tuple-element.52, f32[384]{0:T(512)S(1)} %broadcast_maximum_fusion, s32[1536]{0:T(1024)S(1)} %fusion.38, s32[1536]{0:T(1024)S(1)} %add_select_fusion, s32[384]{0:T(512)S(1)} %get-tuple-element.54, s32[384]{0:T(512)S(1)} %get-tuple-element.53), kind=kLoop, calls=%fused_computation.4 | loop fusion | flops 3538560 | bytes 2377728 | tf_op jit(solution)/shard_map/reduce_sum | solution.py:57
  57.0 0.2 fusion.26
  57.3 0.4 fusion.12
  57.7 0.7 copy.20
  58.3 5.7 %all-to-all-start.1 = ((bf16[8,48,128]{2,1,0:T(8,128)(2,1)}), bf16[8,48,128]{2,1,0:T(8,128)(2,1)S(1)}, u32[]{:S(2)}, u32[]{:S(2)}) async-start(bf16[8,48,128]{2,1,0:T(8,128)(2,1)} %copy.20), calls=%async_computation.1 | async-start | bytes 196608 | tf_op jit(solution)/shard_map/all_to_all | solution.py:35
  64.0 6.0 %all-to-all-done.1 = bf16[8,48,128]{2,1,0:T(8,128)(2,1)S(1)} async-done(((bf16[8,48,128]{2,1,0:T(8,128)(2,1)}), bf16[8,48,128]{2,1,0:T(8,128)(2,1)S(1)}, u32[]{:S(2)}, u32[]{:S(2)}) %all-to-all-start.1) | async-done | bytes 98336 | tf_op jit(solution)/shard_map/all_to_all | solution.py:35
  70.0 7.6 %all_gather.11 = bf16[1536,128]{1,0:T(8,128)(2,1)S(1)} all-gather(bf16[384,128]{1,0:T(8,128)(2,1)S(1)} %bitcast.55), channel_id=1, replica_groups=mesh['tensor'=8,'context'=4] {'context'}, dimensions={0}, use_global_device_ids=true | all-gather | bytes 491520 | tf_op jit(solution)/shard_map/all_gather | solution.py:41
  77.6 3.0 %fusion.17 = bf16[384,128]{1,0:T(8,128)(2,1)} fusion(bf16[1536,128]{1,0:T(8,128)(2,1)S(1)} %all_gather.11, f32[384,1536]{1,0:T(8,128)} %get-tuple-element.52, f32[384]{0:T(512)S(1)} %broadcast_maximum_fusion, s32[1536]{0:T(1024)S(1)} %fusion.38, s32[1536]{0:T(1024)S(1)} %add_select_fusion, s32[384]{0:T(512)S(1)} %get-tuple-element.54, ...), kind=kOutput, calls=%fused_computation.19 | convolution fusion | flops 154681344 | bytes 2870784 | tf_op jit(solution)/shard_map/dot_general | solution.py:58
  (55 shorter events, 0.3 us)
Async XLA Ops:
  0.0 47.5 %copy-start = (bf16[8192,128]{1,0:T(8,128)(2,1)S(1)}, bf16[8192,128]{1,0:T(8,128)(2,1)}, u32[]{:S(2)}) copy-start(bf16[8192,128]{1,0:T(8,128)(2,1)} %param.13) | copy-start | bytes 6291460
  0.0 15.0 %copy-start.23 = (u32[32]{0:T(128)S(1)}, u32[32]{0:T(128)}, u32[]{:S(2)}) copy-start(u32[32]{0:T(128)} %constant.317) | copy-start | bytes 388
  0.0 14.3 %copy-start.1 = (s32[4]{0:T(128)S(1)}, s32[4]{0:T(128)}, u32[]{:S(2)}) copy-start(s32[4]{0:T(128)} %param.19) | copy-start | bytes 52
  7.9 48.9 %all-to-all-start = ((bf16[8,2,3072]{2,1,0:T(2,128)(2,1)}), bf16[8,2,3072]{2,1,0:T(2,128)(2,1)S(1)}, u32[]{:S(2)}, u32[]{:S(2)}) async-start(bf16[8,2,3072]{2,1,0:T(2,128)(2,1)} %reshape.320), calls=%async_computation | async-start | bytes 196608 | tf_op jit(solution)/shard_map/all_to_all | solution.py:30
  22.1 12.5 %copy-start.18 = (pred[384]{0:T(512)(128)(4,1)S(1)}, pred[384]{0:T(512)(128)(4,1)}, u32[]{:S(2)}) copy-start(pred[384]{0:T(512)(128)(4,1)} %constant.309) | copy-start | bytes 1156
  22.2 12.5 %copy-start.19 = (pred[384]{0:T(512)(128)(4,1)S(1)}, pred[384]{0:T(512)(128)(4,1)}, u32[]{:S(2)}) copy-start(pred[384]{0:T(512)(128)(4,1)} %constant.310) | copy-start | bytes 1156
  22.2 12.5 %copy-start.20 = (pred[384]{0:T(512)(128)(4,1)S(1)}, pred[384]{0:T(512)(128)(4,1)}, u32[]{:S(2)}) copy-start(pred[384]{0:T(512)(128)(4,1)} %constant.311) | copy-start | bytes 1156
  22.2 15.0 %copy-start.3 = (pred[1536]{0:T(1024)(128)(4,1)S(1)}, pred[1536]{0:T(1024)(128)(4,1)}, u32[]{:S(2)}) copy-start(pred[1536]{0:T(1024)(128)(4,1)} %constant.292) | copy-start | bytes 4612
  22.2 15.0 %copy-start.4 = (pred[1536]{0:T(1024)(128)(4,1)S(1)}, pred[1536]{0:T(1024)(128)(4,1)}, u32[]{:S(2)}) copy-start(pred[1536]{0:T(1024)(128)(4,1)} %constant.293) | copy-start | bytes 4612
  22.2 15.0 %copy-start.5 = (pred[1536]{0:T(1024)(128)(4,1)S(1)}, pred[1536]{0:T(1024)(128)(4,1)}, u32[]{:S(2)}) copy-start(pred[1536]{0:T(1024)(128)(4,1)} %constant.294) | copy-start | bytes 4612
  22.2 15.0 %copy-start.6 = (pred[1536]{0:T(1024)(128)(4,1)S(1)}, pred[1536]{0:T(1024)(128)(4,1)}, u32[]{:S(2)}) copy-start(pred[1536]{0:T(1024)(128)(4,1)} %constant.295) | copy-start | bytes 4612
  22.2 15.0 %copy-start.7 = (pred[1536]{0:T(1024)(128)(4,1)S(1)}, pred[1536]{0:T(1024)(128)(4,1)}, u32[]{:S(2)}) copy-start(pred[1536]{0:T(1024)(128)(4,1)} %constant.296) | copy-start | bytes 4612
  22.2 15.0 %copy-start.8 = (pred[1536]{0:T(1024)(128)(4,1)S(1)}, pred[1536]{0:T(1024)(128)(4,1)}, u32[]{:S(2)}) copy-start(pred[1536]{0:T(1024)(128)(4,1)} %constant.297) | copy-start | bytes 4612
  22.3 15.0 %copy-start.9 = (pred[1536]{0:T(1024)(128)(4,1)S(1)}, pred[1536]{0:T(1024)(128)(4,1)}, u32[]{:S(2)}) copy-start(pred[1536]{0:T(1024)(128)(4,1)} %constant.298) | copy-start | bytes 4612
  22.3 15.0 %copy-start.10 = (pred[1536]{0:T(1024)(128)(4,1)S(1)}, pred[1536]{0:T(1024)(128)(4,1)}, u32[]{:S(2)}) copy-start(pred[1536]{0:T(1024)(128)(4,1)} %constant.299) | copy-start | bytes 4612
  22.3 15.0 %copy-start.11 = (pred[1536]{0:T(1024)(128)(4,1)S(1)}, pred[1536]{0:T(1024)(128)(4,1)}, u32[]{:S(2)}) copy-start(pred[1536]{0:T(1024)(128)(4,1)} %constant.300) | copy-start | bytes 4612
  22.3 15.0 %copy-start.12 = (pred[1536]{0:T(1024)(128)(4,1)S(1)}, pred[1536]{0:T(1024)(128)(4,1)}, u32[]{:S(2)}) copy-start(pred[1536]{0:T(1024)(128)(4,1)} %constant.301) | copy-start | bytes 4612
  22.3 15.0 %copy-start.13 = (pred[1536]{0:T(1024)(128)(4,1)S(1)}, pred[1536]{0:T(1024)(128)(4,1)}, u32[]{:S(2)}) copy-start(pred[1536]{0:T(1024)(128)(4,1)} %constant.302) | copy-start | bytes 4612
  22.3 15.0 %copy-start.14 = (pred[1536]{0:T(1024)(128)(4,1)S(1)}, pred[1536]{0:T(1024)(128)(4,1)}, u32[]{:S(2)}) copy-start(pred[1536]{0:T(1024)(128)(4,1)} %constant.303) | copy-start | bytes 4612
  22.3 15.0 %copy-start.15 = (pred[1536]{0:T(1024)(128)(4,1)S(1)}, pred[1536]{0:T(1024)(128)(4,1)}, u32[]{:S(2)}) copy-start(pred[1536]{0:T(1024)(128)(4,1)} %constant.304) | copy-start | bytes 4612
  22.4 15.0 %copy-start.16 = (pred[1536]{0:T(1024)(128)(4,1)S(1)}, pred[1536]{0:T(1024)(128)(4,1)}, u32[]{:S(2)}) copy-start(pred[1536]{0:T(1024)(128)(4,1)} %constant.305) | copy-start | bytes 4612
  22.4 15.0 %copy-start.17 = (pred[1536]{0:T(1024)(128)(4,1)S(1)}, pred[1536]{0:T(1024)(128)(4,1)}, u32[]{:S(2)}) copy-start(pred[1536]{0:T(1024)(128)(4,1)} %constant.306) | copy-start | bytes 4612
  54.4 2.9 %copy-start.22 = (bf16[8,16]{1,0:T(8,128)(2,1)S(1)}, bf16[8,16]{1,0:T(8,128)(2,1)}, u32[]{:S(2)}) copy-start(bf16[8,16]{1,0:T(8,128)(2,1)} %param.17) | copy-start | bytes 772
  58.3 11.7 %all-to-all-start.1 = ((bf16[8,48,128]{2,1,0:T(8,128)(2,1)}), bf16[8,48,128]{2,1,0:T(8,128)(2,1)S(1)}, u32[]{:S(2)}, u32[]{:S(2)}) async-start(bf16[8,48,128]{2,1,0:T(8,128)(2,1)} %copy.20), calls=%async_computation.1 | async-start | bytes 196608 | tf_op jit(solution)/shard_map/all_to_all | solution.py:35
  (2 other events, 5.4 us)
where the time goes:
time: 81.3 us; the launch traced here: 80.6 us
  matrix products  21.2 us (26%)
  blocking collectives  19.4 us (24%)
  other arithmetic  16.3 us (20%)
  starting transfers between devices  12.1 us (15%)
  waiting for transfers between devices  5.97 us (7%)
  local copies, waits for them, and re-layouts  4.51 us (6%)
  between operations  1.11 us (1%)
    add x1, other arithmetic, shards(): jnp.repeat(block_all, BLK, total_repeat_length=count) * BLK + offsets % BLK  10.1 us
    all_gather x1, blocking collectives, shards(): value_piece = lax.all_gather(mixed_rows, 'context', axis=0, tiled=True)  7.56 us
    all_gather x1, blocking collectives, shards(): key_piece = lax.all_gather(key_rows, 'context', axis=0, tiled=True)  7.05 us
    dot_general x1, matrix products, shards(): lax.dot_general(query_rows, key_piece, (((1,), (1,)), ((), ())), preferre...  6.95 us
    all_to_all x1, starting transfers between devices, shards(): lax.all_to_all(value_rows[None], 'tensor', split_axis=1, concat_axis=0, t...  6.38 us
    all_to_all x1, waiting for transfers between devices, shards(): lax.all_to_all(mixed_here, 'tensor', split_axis=0, concat_axis=1, tiled=T...  5.97 us
    all_to_all x1, starting transfers between devices, shards(): lax.all_to_all(mixed_here, 'tensor', split_axis=0, concat_axis=1, tiled=T...  5.71 us
    dot_general x1, matrix products, shards(): jnp.dot(tokens, w_value, preferred_element_type=jnp.float32)  5.36 us
  transfers between devices with their start and end apart: 2, of which 1 were waited for; matrix products, arithmetic and copies ran while one was open for 37% of the time, Pallas kernels for 0%

commit v1 on v0

v1 whole, which is shorter than its diff:
```python
import functools

import jax
import jax.numpy as jnp
from jax import lax
from jax.experimental import pallas as pl
from jax.experimental.pallas import tpu as pltpu
from jax.sharding import PartitionSpec as P

HEAD_DIM = 128
BLK = 96
SEQS = 2
MESH = pl.DeviceIdType.MESH
F32 = jnp.float32
BF16 = jnp.bfloat16


def flat_rows(x):
    rows = x.size // x.shape[-1]
    if x.shape[-2] % 16:
        return x.astype(F32).reshape(rows, x.shape[-1]).astype(x.dtype)
    return x.reshape(rows, x.shape[-1])


def picks(shape, row_div, col_div):
    row = lax.broadcasted_iota(jnp.int32, shape, 0) // row_div
    col = lax.broadcasted_iota(jnp.int32, shape, 1) // col_div
    return (row == col).astype(F32)


def spread(small, step):
    tall, wide = small.shape[0] * step, small.shape[1] * step
    lifted = jnp.dot(
        picks((tall, small.shape[0]), step, 1), small, preferred_element_type=F32
    )
    lifted = jnp.dot(
        lifted, picks((small.shape[1], wide), 1, step), preferred_element_type=F32
    )
    row = lax.broadcasted_iota(jnp.int32, (tall, wide), 0) % step
    col = lax.broadcasted_iota(jnp.int32, (tall, wide), 1) % step
    return jnp.where(row == col, lifted, 0.0).astype(BF16)


def kernel(
    heads, ctx, parts,
    ids_ref, x_ref, wq_ref, wk_ref, wv_ref, gate_ref, up_ref, down_ref, out_ref,
    xbuf, wvbuf, wkqbuf, gubuf, dnbuf, vsend, vrecv, msend, mbuf, kbuf, qbuf, idbuf, pbuf, tbuf,
    load_sem, vs_sem, vr_sem, ms_sem, mr_sem, ks_sem, kr_sem, is_sem, ir_sem, cs_sem, cr_sem,
):
    ti = lax.axis_index("tensor")
    ci = lax.axis_index("context")
    rows, depth = x_ref.shape
    step = depth // parts
    slab = rows // heads
    seq_rows = rows // SEQS

    loads = []

    def load(src, dst):
        copy = pltpu.make_async_copy(src, dst, load_sem.at[len(loads)])
        copy.start()
        loads.append(copy)
        return copy

    v_loads, kq_loads = [], []
    for i in range(parts):
        ks = pl.ds(i * step, step)
        v_loads.append(
            (load(x_ref.at[:, ks], xbuf.at[:, ks]), load(wv_ref.at[ks, :], wvbuf.at[ks, :]))
        )
    for i in range(parts):
        ks = pl.ds(i * step, step)
        kq_loads.append(
            (
                load(wk_ref.at[ks, :], wkqbuf.at[ks, 0:HEAD_DIM]),
                load(wq_ref.at[ks, :], wkqbuf.at[ks, HEAD_DIM : 2 * HEAD_DIM]),
            )
        )

    barrier = pltpu.get_barrier_semaphore()
    for d in range(1, heads):
        pl.semaphore_signal(
            barrier, inc=1, device_id={"tensor": lax.rem(ti + d, heads)}, device_id_type=MESH
        )
    for d in range(1, ctx):
        pl.semaphore_signal(
            barrier, inc=1, device_id={"context": lax.rem(ci + d, ctx)}, device_id_type=MESH
        )

    tile = 16 if slab % 16 == 0 else slab
    half = gate_ref.shape[1] * tile
    gubuf[0:half] = spread(gate_ref[...].astype(F32).T, tile)
    gubuf[half : 2 * half] = spread(up_ref[...].astype(F32).T, tile)
    dnbuf[...] = spread(down_ref[...].astype(F32).T, tile)

    sub = lax.broadcasted_iota(jnp.int32, (8, 128), 0)
    own_ids = jnp.zeros((8, 128), jnp.int32)
    for b in range(2 * SEQS):
        own_ids = jnp.where(sub == b, ids_ref[b], own_ids)
    idbuf[ci] = own_ids

    acc = jnp.zeros((rows, HEAD_DIM), F32)
    for i in range(parts):
        for copy in v_loads[i]:
            copy.wait()
        ks = slice(i * step, (i + 1) * step)
        acc += jnp.dot(xbuf[:, ks], wvbuf[ks, :], preferred_element_type=F32)
    if slab % 16:
        vsend[...] = acc.reshape(heads, slab, HEAD_DIM).astype(BF16)
    else:
        vsend[...] = acc.astype(BF16).reshape(heads, slab, HEAD_DIM)

    pl.semaphore_wait(barrier, heads - 1 + ctx - 1)

    v_copies = []
    for d in range(1, heads):
        peer = lax.rem(ti + d, heads)
        copy = pltpu.make_async_remote_copy(
            src_ref=vsend.at[peer], dst_ref=vrecv.at[ti],
            send_sem=vs_sem.at[d], recv_sem=vr_sem.at[ti],
            device_id={"tensor": peer}, device_id_type=MESH,
        )
        copy.start()
        v_copies.append(copy)
    i_copies = []
    for d in range(1, ctx):
        peer = lax.rem(ci + d, ctx)
        copy = pltpu.make_async_remote_copy(
            src_ref=idbuf.at[ci], dst_ref=idbuf.at[ci],
            send_sem=is_sem.at[d], recv_sem=ir_sem.at[ci],
            device_id={"context": peer}, device_id_type=MESH,
        )
        copy.start()
        i_copies.append(copy)
    vrecv[ti] = vsend[ti]

    acc = jnp.zeros((rows, 2 * HEAD_DIM), F32)
    for i in range(parts):
        for copy in kq_loads[i]:
            copy.wait()
        ks = slice(i * step, (i + 1) * step)
        acc += jnp.dot(xbuf[:, ks], wkqbuf[ks, :], preferred_element_type=F32)
    kbuf[ci] = acc[:, :HEAD_DIM].astype(BF16).reshape(SEQS, seq_rows, HEAD_DIM)
    k_copies = []
    for d in range(1, ctx):
        peer = lax.rem(ci + d, ctx)
        copy = pltpu.make_async_remote_copy(
            src_ref=kbuf.at[ci], dst_ref=kbuf.at[ci],
            send_sem=ks_sem.at[d], recv_sem=kr_sem.at[ci],
            device_id={"context": peer}, device_id_type=MESH,
        )
        copy.start()
        k_copies.append(copy)
    qbuf[...] = acc[:, HEAD_DIM:].astype(BF16)

    for d in range(1, heads):
        src = lax.rem(ti + d, heads)
        pltpu.make_async_remote_copy(
            src_ref=vsend.at[src], dst_ref=vrecv.at[src],
            send_sem=vs_sem.at[d], recv_sem=vr_sem.at[src],
            device_id={"tensor": src}, device_id_type=MESH,
        ).wait_recv()
    pieces = slab // tile
    x = jnp.concatenate(
        [flat_rows(vrecv[:, j * tile : (j + 1) * tile, :]) for j in range(pieces)], axis=1
    )
    both = jnp.dot(gubuf[...], x, preferred_element_type=F32)
    hidden = (jax.nn.silu(both[:half]) * both[half:]).astype(BF16)
    mixed = x.astype(F32) + jnp.dot(dnbuf[...], hidden, preferred_element_type=F32)
    for j in range(pieces):
        piece = mixed[:, j * HEAD_DIM : (j + 1) * HEAD_DIM]
        if tile % 16:
            piece = piece.reshape(heads, tile, HEAD_DIM).astype(BF16)
        else:
            piece = piece.astype(BF16).reshape(heads, tile, HEAD_DIM)
        msend[:, j * tile : (j + 1) * tile, :] = piece
    m_copies = []
    for d in range(1, heads):
        peer = lax.rem(ti + d, heads)
        copy = pltpu.make_async_remote_copy(
            src_ref=msend.at[peer], dst_ref=mbuf.at[ci, ti],
            send_sem=ms_sem.at[d], recv_sem=mr_sem.at[ti],
            device_id={"tensor": peer}, device_id_type=MESH,
        )
        copy.start()
        m_copies.append(copy)
    mbuf[ci, ti] = msend[ti]

    for d in range(1, ctx):
        src = lax.rem(ci + d, ctx)
        pltpu.make_async_remote_copy(
            src_ref=idbuf.at[src], dst_ref=idbuf.at[src],
            send_sem=is_sem.at[d], recv_sem=ir_sem.at[src],
            device_id={"context": src}, device_id_type=MESH,
        ).wait_recv()
    for d in range(1, ctx):
        src = lax.rem(ci + d, ctx)
        pltpu.make_async_remote_copy(
            src_ref=kbuf.at[src], dst_ref=kbuf.at[src],
            send_sem=ks_sem.at[d], recv_sem=kr_sem.at[src],
            device_id={"context": src}, device_id_type=MESH,
        ).wait_recv()
    scale = HEAD_DIM ** (-0.5)
    count = ctx * seq_rows
    lane = lax.broadcasted_iota(jnp.int32, (1, count), 1)
    row = lax.broadcasted_iota(jnp.int32, (seq_rows, 1), 0)
    for s in range(SEQS):
        key_pos = jnp.zeros((1, count), jnp.int32)
        for c in range(ctx):
            ids = idbuf[c]
            for b in range(2):
                r = 2 * s + b
                wide = jnp.concatenate([ids[r : r + 1, :]] * (count // 128), axis=1)
                key_pos = jnp.where(lane // BLK == 2 * c + b, wide, key_pos)
        key_pos = key_pos * BLK + lane % BLK
        query_pos = (
            jnp.where(row < BLK, ids_ref[2 * s], ids_ref[2 * s + 1]) * BLK + row % BLK
        )
        keys = kbuf[:, s].reshape(count, HEAD_DIM)
        scores = lax.dot_general(
            qbuf[s * seq_rows : (s + 1) * seq_rows, :], keys,
            (((1,), (1,)), ((), ())), preferred_element_type=F32,
        ) * scale
        scores = jnp.where(key_pos <= query_pos, scores, -1e30)
        weights = jnp.exp(scores - jnp.max(scores, axis=1, keepdims=True))
        tbuf[s] = jnp.broadcast_to(jnp.sum(weights, axis=1, keepdims=True), (seq_rows, HEAD_DIM))
        pbuf[s] = weights.astype(BF16)

    for d in range(1, heads):
        src = lax.rem(ti + d, heads)
        pltpu.make_async_remote_copy(
            src_ref=msend.at[src], dst_ref=mbuf.at[ci, src],
            send_sem=ms_sem.at[d], recv_sem=mr_sem.at[src],
            device_id={"tensor": src}, device_id_type=MESH,
        ).wait_recv()
    c_copies = []
    for d in range(1, ctx):
        peer = lax.rem(ci + d, ctx)
        copy = pltpu.make_async_remote_copy(
            src_ref=mbuf.at[ci], dst_ref=mbuf.at[ci],
            send_sem=cs_sem.at[d], recv_sem=cr_sem.at[ci],
            device_id={"context": peer}, device_id_type=MESH,
        )
        copy.start()
        c_copies.append(copy)
    for d in range(1, ctx):
        src = lax.rem(ci + d, ctx)
        pltpu.make_async_remote_copy(
            src_ref=mbuf.at[src], dst_ref=mbuf.at[src],
            send_sem=cs_sem.at[d], recv_sem=cr_sem.at[src],
            device_id={"context": src}, device_id_type=MESH,
        ).wait_recv()
    per_seq = heads // SEQS
    for s in range(SEQS):
        values = flat_rows(mbuf[:, s * per_seq : (s + 1) * per_seq])
        summed = jnp.dot(pbuf[s], values, preferred_element_type=F32)
        out_ref[s * seq_rows : (s + 1) * seq_rows, :] = (summed / tbuf[s]).astype(BF16)

    for copy in v_copies + i_copies + k_copies + m_copies + c_copies:
        copy.wait_send()


def solution(mesh):
    heads, ctx = mesh.shape["tensor"], mesh.shape["context"]

    def shards(tokens, w_query, w_key, w_value, mix_gate, mix_up, mix_down, block_ids):
        rows, depth = tokens.shape
        slab = rows // heads
        seq_rows = rows // SEQS
        tile = 16 if slab % 16 == 0 else slab
        mixf = mix_gate.shape[1]
        parts = 8
        dma = pltpu.SemaphoreType.DMA
        vmem = pl.BlockSpec(memory_space=pltpu.VMEM)
        hbm = pl.BlockSpec(memory_space=pl.ANY)
        return pl.pallas_call(
            functools.partial(kernel, heads, ctx, parts),
            out_shape=jax.ShapeDtypeStruct((rows, HEAD_DIM), BF16),
            in_specs=[pl.BlockSpec(memory_space=pltpu.SMEM)] + [hbm] * 4 + [vmem] * 3,
            out_specs=vmem,
            scratch_shapes=[
                pltpu.VMEM((rows, depth), BF16),
                pltpu.VMEM((depth, HEAD_DIM), BF16),
                pltpu.VMEM((depth, 2 * HEAD_DIM), BF16),
                pltpu.VMEM((2 * mixf * tile, heads * tile), BF16),
                pltpu.VMEM((heads * tile, mixf * tile), BF16),
                pltpu.VMEM((heads, slab, HEAD_DIM), BF16),
                pltpu.VMEM((heads, slab, HEAD_DIM), BF16),
                pltpu.VMEM((heads, slab, HEAD_DIM), BF16),
                pltpu.VMEM((ctx, heads, slab, HEAD_DIM), BF16),
                pltpu.VMEM((ctx, SEQS, seq_rows, HEAD_DIM), BF16),
                pltpu.VMEM((rows, HEAD_DIM), BF16),
                pltpu.VMEM((ctx, 8, 128), jnp.int32),
                pltpu.VMEM((SEQS, seq_rows, ctx * seq_rows), BF16),
                pltpu.VMEM((SEQS, seq_rows, HEAD_DIM), F32),
                dma((4 * parts,)),
                dma((heads,)), dma((heads,)), dma((heads,)), dma((heads,)),
                dma((ctx,)), dma((ctx,)), dma((ctx,)), dma((ctx,)), dma((ctx,)), dma((ctx,)),
            ],
            compiler_params=pltpu.CompilerParams(
                collective_id=0, has_side_effects=True, vmem_limit_bytes=48 * 2**20
            ),
        )(block_ids, tokens, w_query, w_key, w_value, mix_gate, mix_up, mix_down)

    in_specs = (
        P("context", None),
        P(None, "tensor"),
        P(None, "tensor"),
        P(None, "tensor"),
        P(),
        P(),
        P(),
        P("context"),
    )
    out_specs = P("context", "tensor")
    return jax.shard_map(shards, mesh=mesh, in_specs=in_specs, out_specs=out_specs, check_vma=False)
```

time: 81.3 us -> 30.8 us (0.38)
  Pallas kernels: 0 us -> 23.9 us
  matrix products: 21.2 us -> 0 us
  blocking collectives: 19.4 us -> 0 us
  other arithmetic: 16.3 us -> 0 us
  starting transfers between devices: 12.1 us -> 0 us
  waiting for transfers between devices: 5.97 us -> 0 us
  local copies, waits for them, and re-layouts: 4.51 us -> 6.6 us
  between operations: 1.11 us -> 0.01 us
    pallas_call x0 -> x1, Pallas kernels: none -> 23.9 us  [shards(): pl.pallas_call(functools.partial(kernel, heads, ctx, parts), out_shape=ja...]
    dot_general x6 -> x0, matrix products: 21.2 us -> none  [the longest x1 6.95 us: shards(): lax.dot_general(query_rows, key_piece, (((1,), (1,)), ((), ())), preferre...]
    all_gather x2 -> x0, blocking collectives: 14.6 us -> none  [the longest x1 7.56 us: shards(): value_piece = lax.all_gather(mixed_rows, 'context', axis=0, tiled=True)]
    all_to_all x2 -> x0, starting transfers between devices: 12.1 us -> none  [the longest x1 6.38 us: shards(): lax.all_to_all(value_rows[None], 'tensor', split_axis=1, concat_axis=0, t...]
    add x1 -> x0, other arithmetic: 10.1 us -> none  [shards(): jnp.repeat(block_all, BLK, total_repeat_length=count) * BLK + offsets % BLK]
    all_to_all x2 -> x0, waiting for transfers between devices: 5.97 us -> none  [the longest x1 5.97 us: shards(): lax.all_to_all(mixed_here, 'tensor', split_axis=0, concat_axis=1, tiled=T...]
    unnamed x1 -> x0, blocking collectives: 4.8 us -> none
    unnamed x55 -> x12, local copies, waits for them, and re-layouts: 2.33 us -> 6.6 us
  transfers between devices with their start and end apart: 2 -> 0, of which waited for: 1 -> 0; matrix products, arithmetic and copies ran while one was open for 37% -> 0% of each run, Pallas kernels for 0% -> 0%
where the time goes in v1:
time: 30.8 us; the launch traced here: 30.6 us
  Pallas kernels  23.9 us (78%)
  local copies, waits for them, and re-layouts  6.6 us (21%)
    pallas_call x1, Pallas kernels, shards(): pl.pallas_call(functools.partial(kernel, heads, ctx, parts), out_shape=ja...  23.9 us
    unnamed x12, local copies, waits for them, and re-layouts  6.6 us

profile of v1, /device:TPU:1, one launch (start us, length us, event | category | flops | bytes accessed | tf_op | source)
XLA Modules:
  0.0 30.6 jit_solution(18342052151220659243)
XLA Ops:
  0.0 0.8 %copy.9.down_ref = bf16[16,8]{1,0:T(8,128)(2,1)S(1)} copy(bf16[16,8]{0,1:T(8,128)(2,1)} %param.14) | data formatting | bytes 512 | tf_op args[6]
  0.8 0.0 copy-start
  0.8 1.6 %copy-done = bf16[8192,128]{1,0:T(8,128)(2,1)S(1)} copy-done((bf16[8192,128]{1,0:T(8,128)(2,1)S(1)}, bf16[8192,128]{1,0:T(8,128)(2,1)}, u32[]{:S(2)}) %copy-start) | copy-done | bytes 2097176
  2.4 0.0 copy-start.1
  2.4 1.6 %copy-done.1 = bf16[8192,128]{1,0:T(8,128)(2,1)S(1)} copy-done((bf16[8192,128]{1,0:T(8,128)(2,1)S(1)}, bf16[8192,128]{1,0:T(8,128)(2,1)}, u32[]{:S(2)}) %copy-start.1) | copy-done | bytes 2097176
  3.9 0.0 copy-start.2
  3.9 0.7 %copy-done.2 = bf16[8,16]{1,0:T(8,128)(2,1)S(1)} copy-done((bf16[8,16]{1,0:T(8,128)(2,1)S(1)}, bf16[8,16]{1,0:T(8,128)(2,1)}, u32[]{:S(2)}) %copy-start.2) | copy-done | bytes 280
  4.6 0.0 copy-start.3
  4.6 0.7 %copy-done.3 = bf16[8,16]{1,0:T(8,128)(2,1)S(1)} copy-done((bf16[8,16]{1,0:T(8,128)(2,1)S(1)}, bf16[8,16]{1,0:T(8,128)(2,1)}, u32[]{:S(2)}) %copy-start.3) | copy-done | bytes 280
  5.3 0.0 copy-start.4
  5.3 0.7 %copy-done.4 = s32[4]{0:T(128)S(1)} copy-done((s32[4]{0:T(128)S(1)}, s32[4]{0:T(128)}, u32[]{:S(2)}) %copy-start.4) | copy-done | bytes 40
  6.0 23.9 %shard_map.82 = bf16[384,128]{1,0:T(8,128)(2,1)S(1)} custom-call(s32[4]{0:T(128)S(1)} %copy-done.4, bf16[384,8192]{1,0:T(8,128)(2,1)} %x_ref.1, bf16[8192,128]{1,0:T(8,128)(2,1)S(1)} %copy-done, bf16[8192,128]{1,0:T(8,128)(2,1)S(1)} %copy-done.1, bf16[8192,128]{1,0:T(8,128)(2,1)} %wv_ref.1, bf16[8,16]{1,0:T(8,128)(2,1)S(1)} %copy-done.2, ...), custom_call_target="tpu_custom_call" | custom-call | tf_op jit(solution)/shard_map/pallas_call | solution.py:276
  29.9 0.6 %copy.11 = bf16[384,128]{1,0:T(8,128)(2,1)} copy(bf16[384,128]{1,0:T(8,128)(2,1)S(1)} %shard_map.82) | data formatting | bytes 196608
Async XLA Ops:
  0.8 1.6 %copy-start = (bf16[8192,128]{1,0:T(8,128)(2,1)S(1)}, bf16[8192,128]{1,0:T(8,128)(2,1)}, u32[]{:S(2)}) copy-start(bf16[8192,128]{1,0:T(8,128)(2,1)} %wq_ref.1) | copy-start | bytes 6291460
  2.4 1.6 %copy-start.1 = (bf16[8192,128]{1,0:T(8,128)(2,1)S(1)}, bf16[8192,128]{1,0:T(8,128)(2,1)}, u32[]{:S(2)}) copy-start(bf16[8192,128]{1,0:T(8,128)(2,1)} %wk_ref.1) | copy-start | bytes 6291460
  3.9 0.7 %copy-start.2 = (bf16[8,16]{1,0:T(8,128)(2,1)S(1)}, bf16[8,16]{1,0:T(8,128)(2,1)}, u32[]{:S(2)}) copy-start(bf16[8,16]{1,0:T(8,128)(2,1)} %gate_ref.1) | copy-start | bytes 772
  4.6 0.7 %copy-start.3 = (bf16[8,16]{1,0:T(8,128)(2,1)S(1)}, bf16[8,16]{1,0:T(8,128)(2,1)}, u32[]{:S(2)}) copy-start(bf16[8,16]{1,0:T(8,128)(2,1)} %up_ref.1) | copy-start | bytes 772
  5.3 0.7 %copy-start.4 = (s32[4]{0:T(128)S(1)}, s32[4]{0:T(128)}, u32[]{:S(2)}) copy-start(s32[4]{0:T(128)} %ids_ref.1) | copy-start | bytes 52

commit v2 on v1

--- a/solution.py
+++ b/solution.py
@@ -43,7 +43,8 @@
 
 def kernel(
     heads, ctx, parts,
-    ids_ref, x_ref, wq_ref, wk_ref, wv_ref, gate_ref, up_ref, down_ref, out_ref,
+    ids_hbm, x_ref, wq_ref, wk_ref, wv_ref, gate_hbm, up_hbm, down_hbm, out_ref,
+    ids_ref, gate_ref, up_ref, down_ref,
     xbuf, wvbuf, wkqbuf, gubuf, dnbuf, vsend, vrecv, msend, mbuf, kbuf, qbuf, idbuf, pbuf, tbuf,
     load_sem, vs_sem, vr_sem, ms_sem, mr_sem, ks_sem, kr_sem, is_sem, ir_sem, cs_sem, cr_sem,
 ):
@@ -54,6 +55,26 @@
     slab = rows // heads
     seq_rows = rows // SEQS
 
+    pairs = ctx // 2
+    sib = ci + 1 - 2 * lax.rem(ci, 2)
+
+    def far(d):
+        return lax.rem(ci + 2 * d, ctx)
+
+    def share(ref, peer, send, recv):
+        copy = pltpu.make_async_remote_copy(
+            src_ref=ref, dst_ref=ref, send_sem=send, recv_sem=recv,
+            device_id={"context": peer}, device_id_type=MESH,
+        )
+        copy.start()
+        return copy
+
+    def arrived(ref, recv):
+        pltpu.make_async_remote_copy(
+            src_ref=ref, dst_ref=ref, send_sem=ks_sem.at[0], recv_sem=recv,
+            device_id={"context": sib}, device_id_type=MESH,
+        ).wait_recv()
+
     loads = []
 
     def load(src, dst):
@@ -62,6 +83,9 @@
         loads.append(copy)
         return copy
 
+    small_loads = [
+        load(gate_hbm, gate_ref), load(up_hbm, up_ref), load(down_hbm, down_ref), load(ids_hbm, ids_ref)
+    ]
     v_loads, kq_loads = [], []
     for i in range(parts):
         ks = pl.ds(i * step, step)
@@ -87,11 +111,14 @@
             barrier, inc=1, device_id={"context": lax.rem(ci + d, ctx)}, device_id_type=MESH
         )
 
+    for copy in small_loads:
+        copy.wait()
+
     tile = 16 if slab % 16 == 0 else slab
     half = gate_ref.shape[1] * tile
     gubuf[0:half] = spread(gate_ref[...].astype(F32).T, tile)
     gubuf[half : 2 * half] = spread(up_ref[...].astype(F32).T, tile)
-    dnbuf[...] = spread(down_ref[...].astype(F32).T, tile)
+    dnbuf[...] = spread(down_ref[...].astype(F32), tile)
 
     sub = lax.broadcasted_iota(jnp.int32, (8, 128), 0)
     own_ids = jnp.zeros((8, 128), jnp.int32)
@@ -141,16 +168,9 @@
         ks = slice(i * step, (i + 1) * step)
         acc += jnp.dot(xbuf[:, ks], wkqbuf[ks, :], preferred_element_type=F32)
     kbuf[ci] = acc[:, :HEAD_DIM].astype(BF16).reshape(SEQS, seq_rows, HEAD_DIM)
-    k_copies = []
-    for d in range(1, ctx):
-        peer = lax.rem(ci + d, ctx)
-        copy = pltpu.make_async_remote_copy(
-            src_ref=kbuf.at[ci], dst_ref=kbuf.at[ci],
-            send_sem=ks_sem.at[d], recv_sem=kr_sem.at[ci],
-            device_id={"context": peer}, device_id_type=MESH,
-        )
-        copy.start()
-        k_copies.append(copy)
+    k_copies = [share(kbuf.at[ci], sib, ks_sem.at[0], kr_sem.at[ci])]
+    for d in range(1, pairs):
+        k_copies.append(share(kbuf.at[ci], far(d), ks_sem.at[d], kr_sem.at[ci]))
     qbuf[...] = acc[:, HEAD_DIM:].astype(BF16)
 
     for d in range(1, heads):
@@ -186,20 +206,36 @@
         m_copies.append(copy)
     mbuf[ci, ti] = msend[ti]
 
+    for d in range(1, pairs):
+        arrived(kbuf.at[far(d)], kr_sem.at[far(d)])
+        k_copies.append(share(kbuf.at[far(d)], sib, ks_sem.at[pairs - 1 + d], kr_sem.at[far(d)]))
+
+    per_seq = heads // SEQS
+    halves = [pl.ds(s * per_seq, per_seq) for s in range(SEQS)]
+    c_copies = []
+    for s in range(SEQS):
+        for p in range(s * per_seq, (s + 1) * per_seq):
+
+            @pl.when(p != ti)
+            def _(p=p):
+                pltpu.make_async_remote_copy(
+                    src_ref=msend.at[p], dst_ref=mbuf.at[ci, p],
+                    send_sem=ms_sem.at[0], recv_sem=mr_sem.at[p],
+                    device_id={"tensor": p}, device_id_type=MESH,
+                ).wait_recv()
+
+        own = mbuf.at[ci, halves[s]]
+        for d in range(1, pairs):
+            c_copies.append(share(own, far(d), cs_sem.at[s, d], cr_sem.at[s, ci]))
+        c_copies.append(share(own, sib, cs_sem.at[s, 0], cr_sem.at[s, ci]))
+
     for d in range(1, ctx):
         src = lax.rem(ci + d, ctx)
-        pltpu.make_async_remote_copy(
-            src_ref=idbuf.at[src], dst_ref=idbuf.at[src],
-            send_sem=is_sem.at[d], recv_sem=ir_sem.at[src],
-            device_id={"context": src}, device_id_type=MESH,
-        ).wait_recv()
-    for d in range(1, ctx):
-        src = lax.rem(ci + d, ctx)
-        pltpu.make_async_remote_copy(
-            src_ref=kbuf.at[src], dst_ref=kbuf.at[src],
-            send_sem=ks_sem.at[d], recv_sem=kr_sem.at[src],
-            device_id={"context": src}, device_id_type=MESH,
-        ).wait_recv()
+        arrived(idbuf.at[src], ir_sem.at[src])
+    arrived(kbuf.at[sib], kr_sem.at[sib])
+    for d in range(1, pairs):
+        there = lax.rem(sib + 2 * d, ctx)
+        arrived(kbuf.at[there], kr_sem.at[there])
     scale = HEAD_DIM ** (-0.5)
     count = ctx * seq_rows
     lane = lax.broadcasted_iota(jnp.int32, (1, count), 1)
@@ -226,32 +262,16 @@
         tbuf[s] = jnp.broadcast_to(jnp.sum(weights, axis=1, keepdims=True), (seq_rows, HEAD_DIM))
         pbuf[s] = weights.astype(BF16)
 
-    for d in range(1, heads):
-        src = lax.rem(ti + d, heads)
-        pltpu.make_async_remote_copy(
-            src_ref=msend.at[src], dst_ref=mbuf.at[ci, src],
-            send_sem=ms_sem.at[d], recv_sem=mr_sem.at[src],
-            device_id={"tensor": src}, device_id_type=MESH,
-        ).wait_recv()
-    c_copies = []
-    for d in range(1, ctx):
-        peer = lax.rem(ci + d, ctx)
-        copy = pltpu.make_async_remote_copy(
-            src_ref=mbuf.at[ci], dst_ref=mbuf.at[ci],
-            send_sem=cs_sem.at[d], recv_sem=cr_sem.at[ci],
-            device_id={"context": peer}, device_id_type=MESH,
-        )
-        copy.start()
-        c_copies.append(copy)
-    for d in range(1, ctx):
-        src = lax.rem(ci + d, ctx)
-        pltpu.make_async_remote_copy(
-            src_ref=mbuf.at[src], dst_ref=mbuf.at[src],
-            send_sem=cs_sem.at[d], recv_sem=cr_sem.at[src],
-            device_id={"context": src}, device_id_type=MESH,
-        ).wait_recv()
-    per_seq = heads // SEQS
     for s in range(SEQS):
+        for d in range(1, pairs):
+            got = mbuf.at[far(d), halves[s]]
+            arrived(got, cr_sem.at[s, far(d)])
+            c_copies.append(share(got, sib, cs_sem.at[s, pairs - 1 + d], cr_sem.at[s, far(d)]))
+    for s in range(SEQS):
+        arrived(mbuf.at[sib, halves[s]], cr_sem.at[s, sib])
+        for d in range(1, pairs):
+            there = lax.rem(sib + 2 * d, ctx)
+            arrived(mbuf.at[there, halves[s]], cr_sem.at[s, there])
         values = flat_rows(mbuf[:, s * per_seq : (s + 1) * per_seq])
         summed = jnp.dot(pbuf[s], values, preferred_element_type=F32)
         out_ref[s * seq_rows : (s + 1) * seq_rows, :] = (summed / tbuf[s]).astype(BF16)
@@ -272,13 +292,17 @@
         parts = 8
         dma = pltpu.SemaphoreType.DMA
         vmem = pl.BlockSpec(memory_space=pltpu.VMEM)
-        hbm = pl.BlockSpec(memory_space=pl.ANY)
+        hbm = pl.BlockSpec(memory_space=pltpu.HBM)
         return pl.pallas_call(
             functools.partial(kernel, heads, ctx, parts),
             out_shape=jax.ShapeDtypeStruct((rows, HEAD_DIM), BF16),
-            in_specs=[pl.BlockSpec(memory_space=pltpu.SMEM)] + [hbm] * 4 + [vmem] * 3,
+            in_specs=[hbm] * 8,
             out_specs=vmem,
             scratch_shapes=[
+                pltpu.SMEM(block_ids.shape, jnp.int32),
+                pltpu.VMEM(mix_gate.shape, BF16),
+                pltpu.VMEM(mix_up.shape, BF16),
+                pltpu.VMEM(mix_down.T.shape, BF16),
                 pltpu.VMEM((rows, depth), BF16),
                 pltpu.VMEM((depth, HEAD_DIM), BF16),
                 pltpu.VMEM((depth, 2 * HEAD_DIM), BF16),
@@ -293,14 +317,14 @@
                 pltpu.VMEM((ctx, 8, 128), jnp.int32),
                 pltpu.VMEM((SEQS, seq_rows, ctx * seq_rows), BF16),
                 pltpu.VMEM((SEQS, seq_rows, HEAD_DIM), F32),
-                dma((4 * parts,)),
+                dma((4 * parts + 4,)),
                 dma((heads,)), dma((heads,)), dma((heads,)), dma((heads,)),
-                dma((ctx,)), dma((ctx,)), dma((ctx,)), dma((ctx,)), dma((ctx,)), dma((ctx,)),
+                dma((ctx,)), dma((ctx,)), dma((ctx,)), dma((ctx,)), dma((SEQS, ctx)), dma((SEQS, ctx)),
             ],
             compiler_params=pltpu.CompilerParams(
-                collective_id=0, has_side_effects=True, vmem_limit_bytes=48 * 2**20
+                collective_id=0, has_side_effects=True, vmem_limit_bytes=56 * 2**20
             ),
-        )(block_ids, tokens, w_query, w_key, w_value, mix_gate, mix_up, mix_down)
+        )(block_ids, tokens, w_query, w_key, w_value, mix_gate, mix_up, mix_down.T)
 
     in_specs = (
         P("context", None),

time: 30.8 us -> 24.9 us (0.81)
  local copies, waits for them, and re-layouts: 6.6 us -> 1.54 us
  Pallas kernels: 23.9 us -> 23.2 us
    unnamed x12 -> x1, local copies, waits for them, and re-layouts: 6.6 us -> 1.54 us
    pallas_call x1, Pallas kernels: 23.9 us -> 23.2 us  [shards(): pl.pallas_call(functools.partial(kernel, heads, ctx, parts), out_shape=ja...]
where the time goes in v2:
time: 24.9 us; the launch traced here: 24.8 us
  Pallas kernels  23.2 us (93%)
  local copies, waits for them, and re-layouts  1.54 us (6%)
    pallas_call x1, Pallas kernels, shards(): pl.pallas_call(functools.partial(kernel, heads, ctx, parts), out_shape=ja...  23.2 us
    unnamed x1, local copies, waits for them, and re-layouts  1.54 us

profile of v2, /device:TPU:1, one launch (start us, length us, event | category | flops | bytes accessed | tf_op | source)
XLA Modules:
  0.0 24.8 jit_solution(1123435889441739306)
XLA Ops:
  0.0 23.2 %shard_map.82 = bf16[384,128]{1,0:T(8,128)(2,1)} custom-call(s32[4]{0:T(128)} %ids_hbm.1, bf16[384,8192]{1,0:T(8,128)(2,1)} %x_ref.1, bf16[8192,128]{1,0:T(8,128)(2,1)} %wq_ref.1, bf16[8192,128]{1,0:T(8,128)(2,1)} %wk_ref.1, bf16[8192,128]{1,0:T(8,128)(2,1)} %wv_ref.1, bf16[8,16]{1,0:T(8,128)(2,1)} %gate_hbm.1, bf16[8,16]{1,0:T(8,128)(2,1)} %up_hbm.1, ...), custom_call_target="tpu_custom_call" | custom-call | tf_op jit(solution)/shard_map/pallas_call | solution.py:296
  23.2 1.5 %copy.10 = bf16[384,128]{1,0:T(8,128)(2,1)} copy(bf16[384,128]{1,0:T(8,128)(2,1)} %shard_map.82) | data formatting | bytes 196608

commit v3 on v2

--- a/solution.py
+++ b/solution.py
@@ -92,7 +92,8 @@
         v_loads.append(
             (load(x_ref.at[:, ks], xbuf.at[:, ks]), load(wv_ref.at[ks, :], wvbuf.at[ks, :]))
         )
-    for i in range(parts):
+
+    def load_kq(i):
         ks = pl.ds(i * step, step)
         kq_loads.append(
             (
@@ -130,6 +131,9 @@
     for i in range(parts):
         for copy in v_loads[i]:
             copy.wait()
+        if i >= parts // 2:
+            load_kq(2 * i - parts)
+            load_kq(2 * i - parts + 1)
         ks = slice(i * step, (i + 1) * step)
         acc += jnp.dot(xbuf[:, ks], wvbuf[ks, :], preferred_element_type=F32)
     if slab % 16:
@@ -139,8 +143,9 @@
 
     pl.semaphore_wait(barrier, heads - 1 + ctx - 1)
 
+    far_first = sorted(range(1, heads), key=lambda d: -min(d, heads - d))
     v_copies = []
-    for d in range(1, heads):
+    for d in far_first:
         peer = lax.rem(ti + d, heads)
         copy = pltpu.make_async_remote_copy(
             src_ref=vsend.at[peer], dst_ref=vrecv.at[ti],
@@ -195,7 +200,7 @@
             piece = piece.astype(BF16).reshape(heads, tile, HEAD_DIM)
         msend[:, j * tile : (j + 1) * tile, :] = piece
     m_copies = []
-    for d in range(1, heads):
+    for d in far_first:
         peer = lax.rem(ti + d, heads)
         copy = pltpu.make_async_remote_copy(
             src_ref=msend.at[peer], dst_ref=mbuf.at[ci, ti],
@@ -211,10 +216,13 @@
         k_copies.append(share(kbuf.at[far(d)], sib, ks_sem.at[pairs - 1 + d], kr_sem.at[far(d)]))
 
     per_seq = heads // SEQS
-    halves = [pl.ds(s * per_seq, per_seq) for s in range(SEQS)]
+    first = ti // per_seq
+    order = [first] + [lax.rem(first + s, SEQS) for s in range(1, SEQS)]
+    halves = [pl.ds(s * per_seq, per_seq) for s in order]
     c_copies = []
-    for s in range(SEQS):
-        for p in range(s * per_seq, (s + 1) * per_seq):
+    for k, s in enumerate(order):
+        for i in range(per_seq):
+            p = s * per_seq + i
 
             @pl.when(p != ti)
             def _(p=p):
@@ -224,10 +232,10 @@
                     device_id={"tensor": p}, device_id_type=MESH,
                 ).wait_recv()
 
-        own = mbuf.at[ci, halves[s]]
+        own = mbuf.at[ci, halves[k]]
         for d in range(1, pairs):
-            c_copies.append(share(own, far(d), cs_sem.at[s, d], cr_sem.at[s, ci]))
-        c_copies.append(share(own, sib, cs_sem.at[s, 0], cr_sem.at[s, ci]))
+            c_copies.append(share(own, far(d), cs_sem.at[k, d], cr_sem.at[k, ci]))
+        c_copies.append(share(own, sib, cs_sem.at[k, 0], cr_sem.at[k, ci]))
 
     for d in range(1, ctx):
         src = lax.rem(ci + d, ctx)
@@ -262,19 +270,19 @@
         tbuf[s] = jnp.broadcast_to(jnp.sum(weights, axis=1, keepdims=True), (seq_rows, HEAD_DIM))
         pbuf[s] = weights.astype(BF16)
 
-    for s in range(SEQS):
+    for k in range(SEQS):
         for d in range(1, pairs):
-            got = mbuf.at[far(d), halves[s]]
-            arrived(got, cr_sem.at[s, far(d)])
-            c_copies.append(share(got, sib, cs_sem.at[s, pairs - 1 + d], cr_sem.at[s, far(d)]))
-    for s in range(SEQS):
-        arrived(mbuf.at[sib, halves[s]], cr_sem.at[s, sib])
+            got = mbuf.at[far(d), halves[k]]
+            arrived(got, cr_sem.at[k, far(d)])
+            c_copies.append(share(got, sib, cs_sem.at[k, pairs - 1 + d], cr_sem.at[k, far(d)]))
+    for k, s in enumerate(order):
+        arrived(mbuf.at[sib, halves[k]], cr_sem.at[k, sib])
         for d in range(1, pairs):
             there = lax.rem(sib + 2 * d, ctx)
-            arrived(mbuf.at[there, halves[s]], cr_sem.at[s, there])
-        values = flat_rows(mbuf[:, s * per_seq : (s + 1) * per_seq])
+            arrived(mbuf.at[there, halves[k]], cr_sem.at[k, there])
+        values = flat_rows(mbuf[:, halves[k]])
         summed = jnp.dot(pbuf[s], values, preferred_element_type=F32)
-        out_ref[s * seq_rows : (s + 1) * seq_rows, :] = (summed / tbuf[s]).astype(BF16)
+        out_ref[pl.ds(pl.multiple_of(s * seq_rows, 16), seq_rows), :] = (summed / tbuf[s]).astype(BF16)
 
     for copy in v_copies + i_copies + k_copies + m_copies + c_copies:
         copy.wait_send()
@@ -295,7 +303,7 @@
         hbm = pl.BlockSpec(memory_space=pltpu.HBM)
         return pl.pallas_call(
             functools.partial(kernel, heads, ctx, parts),
-            out_shape=jax.ShapeDtypeStruct((rows, HEAD_DIM), BF16),
+            out_shape=pltpu.VMEM((rows, HEAD_DIM), BF16),
             in_specs=[hbm] * 8,
             out_specs=vmem,
             scratch_shapes=[

time: 24.9 us -> 24.1 us (0.968)
  local copies, waits for them, and re-layouts: 1.54 us -> 0.64 us
    unnamed x1, local copies, waits for them, and re-layouts: 1.54 us -> 0.64 us
where the time goes in v3:
time: 24.1 us; the launch traced here: 23.9 us
  Pallas kernels  23.3 us (97%)
  local copies, waits for them, and re-layouts  0.64 us (3%)
    pallas_call x1, Pallas kernels, shards(): pl.pallas_call(functools.partial(kernel, heads, ctx, parts), out_shape=pl...  23.3 us
    unnamed x1, local copies, waits for them, and re-layouts  0.64 us

profile of v3, /device:TPU:1, one launch (start us, length us, event | category | flops | bytes accessed | tf_op | source)
XLA Modules:
  0.0 23.9 jit_solution(12989874473333776601)
XLA Ops:
  0.0 23.3 %shard_map.82 = bf16[384,128]{1,0:T(8,128)(2,1)S(1)} custom-call(s32[4]{0:T(128)} %ids_hbm.1, bf16[384,8192]{1,0:T(8,128)(2,1)} %x_ref.1, bf16[8192,128]{1,0:T(8,128)(2,1)} %wq_ref.1, bf16[8192,128]{1,0:T(8,128)(2,1)} %wk_ref.1, bf16[8192,128]{1,0:T(8,128)(2,1)} %wv_ref.1, bf16[8,16]{1,0:T(8,128)(2,1)} %gate_hbm.1, bf16[8,16]{1,0:T(8,128)(2,1)} %up_hbm.1, ...), custom_call_target="tpu_custom_call" | custom-call | tf_op jit(solution)/shard_map/pallas_call | solution.py:304
  23.3 0.6 %copy.10 = bf16[384,128]{1,0:T(8,128)(2,1)} copy(bf16[384,128]{1,0:T(8,128)(2,1)S(1)} %shard_map.82) | data formatting | bytes 196608
